TPU v7x, 512 devices: a whole 4x8x8 slice. The times are simulated.
512 devices in a mesh: dp: 512 (over x, y, z, core).
Axes of the slice: x: 4, y: 8, z: 8, core: 2. Of those that a mesh axis runs over, the one named last changes fastest.
Arguments:
- pooled: bfloat16 [65536, 768], P('dp'), may hold values from -0.19921875 to 0.19921875
- other_part: bfloat16 [65536, 1152], P('dp'), may hold values from -0.19921875 to 0.19921875
- head_weight: bfloat16 [512, 1728], P('dp'), may hold values from -0.21875 to 0.21875
- text: bfloat16 [65536, 1152], P('dp'), may hold values from -0.19921875 to 0.19921875
- logit_scale: float32 [1], replicated, may hold values from 0.5 to 1.5
- logit_bias: float32 [1], replicated, may hold values from -3 to -1
Outputs:
- pooled_grad: bfloat16 [65536, 768], P('dp')
- text_grad: float32 [65536, 1152], P('dp')
- weight_grad: float32 [512, 1728], P('dp')
All inputs are finite; a program needn't handle non-finite values.
Results may differ from a plain program's by a relative error of at most 0.0065.
Values may be sent and summed in bfloat16 or wider, within the bound.
A program may use at most 64 MiB of HBM per device.

v0:
```python
import jax
import jax.numpy as jnp
from jax import lax
from jax.sharding import PartitionSpec as P

D = 1152
KW = 768
WINDOW = 6


def shifted(value, axis, steps):
    count = lax.axis_size(axis)
    pairs = [(source, (source + steps) % count) for source in range(count)]
    return lax.ppermute(value, axis, pairs)


def tile_coef(image_emb, block, offset, temper, bias):
    logits = (
        temper
        * lax.dot_general(
            image_emb, block, (((1,), (1,)), ((), ())), preferred_element_type=jnp.float32
        )
        + bias
    )
    count = image_emb.shape[0]
    if offset == 0:
        label = 2.0 * jnp.eye(count, dtype=jnp.float32) - 1.0
    else:
        label = -jnp.ones((count, count), jnp.float32)
    return (temper * (-label * jax.nn.sigmoid(-label * logits))).astype(jnp.bfloat16)


def pair_tile(image_emb, block, offset, temper, bias):
    coef = tile_coef(image_emb, block, offset, temper, bias)
    image_part = jnp.dot(coef, block, preferred_element_type=jnp.float32)
    text_part = lax.dot_general(
        coef, image_emb, (((0,), (0,)), ((), ())), preferred_element_type=jnp.float32
    )
    return (image_part, text_part)


def body(pooled, other_part, head_weight, text, logit_scale, logit_bias):
    weight = lax.all_gather(head_weight, "dp", axis=0, tiled=True).reshape(KW, D)
    image = jnp.dot(pooled, weight, preferred_element_type=jnp.float32) + other_part.astype(
        jnp.float32
    )
    image_norm = jnp.sqrt(jnp.sum(image * image, axis=1, keepdims=True) + 1e-06)
    image_unit = image / image_norm
    image_emb = image_unit.astype(jnp.bfloat16)
    text_wide = text.astype(jnp.float32)
    text_norm = jnp.sqrt(jnp.sum(text_wide * text_wide, axis=1, keepdims=True) + 1e-06)
    text_unit = text_wide / text_norm
    text_emb = text_unit.astype(jnp.bfloat16)
    temper = jnp.exp(logit_scale[0])
    bias = logit_bias[0]
    half = WINDOW // 2
    current = shifted(text_emb, "dp", -half)
    image_emb_grad = None
    carried = None
    for step in range(WINDOW):
        offset = step - half
        if step > 0:
            current = shifted(current, "dp", 1)
            carried = shifted(carried, "dp", 1)
        image_part, text_part = pair_tile(image_emb, current, offset, temper, bias)
        image_emb_grad = image_part if step == 0 else image_emb_grad + image_part
        carried = text_part if step == 0 else carried + text_part
    text_emb_grad = shifted(carried.astype(jnp.bfloat16), "dp", -(half - 1)).astype(carried.dtype)
    image_grad = (
        (image_emb_grad - image_unit * jnp.sum(image_unit * image_emb_grad, axis=1, keepdims=True))
        / image_norm
    ).astype(jnp.bfloat16)
    pooled_grad = lax.dot_general(
        image_grad, weight, (((1,), (1,)), ((), ())), preferred_element_type=jnp.float32
    ).astype(jnp.bfloat16)
    weight_term = lax.dot_general(
        pooled, image_grad, (((0,), (0,)), ((), ())), preferred_element_type=jnp.float32
    )
    weight_term = weight_term.reshape(lax.axis_size("dp"), -1)
    weight_grad = lax.psum_scatter(weight_term, "dp", scatter_dimension=0, tiled=True)
    text_grad = (
        text_emb_grad - text_unit * jnp.sum(text_unit * text_emb_grad, axis=1, keepdims=True)
    ) / text_norm
    return (pooled_grad, text_grad, weight_grad)


def solution(mesh):
    return jax.shard_map(
        body,
        mesh=mesh,
        in_specs=(P("dp", None), P("dp", None), P("dp", None), P("dp", None), P(), P()),
        out_specs=(P("dp", None), P("dp", None), P("dp", None)),
        check_vma=False,
    )
```

profile of v0, /device:TPU:6, one launch (start us, length us, event | category | flops | bytes accessed | tf_op | source)
XLA Modules:
  0.0 506.5 jit_solution(994258651344585167)
XLA Ops:
  10.2 13.5 %collective-permute-start = (bf16[128,1152]{1,0:T(8,128)(2,1)S(1)}, bf16[128,1152]{1,0:T(8,128)(2,1)S(1)}, u32[]{:S(2)}, u32[]{:S(2)}) collective-permute-start(bf16[128,1152]{1,0:T(8,128)(2,1)S(1)} %fusion.47), channel_id=1, source_target_pairs={{0,509},{1,510},{2,511},{3,0},{4,1},{5,2},{6,3},{7,4},{8,5},{9,6},... | collective-permute-start | bytes 884744 | tf_op jit(solution)/shard_map/ppermute | solution.py:14
  23.7 10.3 %collective-permute-done = bf16[128,1152]{1,0:T(8,128)(2,1)S(1)} collective-permute-done((bf16[128,1152]{1,0:T(8,128)(2,1)S(1)}, bf16[128,1152]{1,0:T(8,128)(2,1)S(1)}, u32[]{:S(2)}, u32[]{:S(2)}) %collective-permute-start) | collective-permute-done | bytes 294944 | tf_op jit(solution)/shard_map/ppermute | solution.py:14
  34.0 2.0 collective-permute-start.1
  36.0 10.3 %collective-permute-done.1 = bf16[128,1152]{1,0:T(8,128)(2,1)S(1)} collective-permute-done((bf16[128,1152]{1,0:T(8,128)(2,1)S(1)}, bf16[128,1152]{1,0:T(8,128)(2,1)S(1)}, u32[]{:S(2)}, u32[]{:S(2)}) %collective-permute-start.1) | collective-permute-done | bytes 294944 | tf_op jit(solution)/shard_map/ppermute | solution.py:14
  48.2 10.3 %collective-permute-done.2 = bf16[128,1152]{1,0:T(8,128)(2,1)S(1)} collective-permute-done((bf16[128,1152]{1,0:T(8,128)(2,1)S(1)}, bf16[128,1152]{1,0:T(8,128)(2,1)S(1)}, u32[]{:S(2)}, u32[]{:S(2)}) %collective-permute-start.2) | collective-permute-done | bytes 294944 | tf_op jit(solution)/shard_map/ppermute | solution.py:14
  60.5 10.4 %collective-permute-done.3 = bf16[128,1152]{1,0:T(8,128)(2,1)S(1)} collective-permute-done((bf16[128,1152]{1,0:T(8,128)(2,1)S(1)}, bf16[128,1152]{1,0:T(8,128)(2,1)S(1)}, u32[]{:S(2)}, u32[]{:S(2)}) %collective-permute-start.3) | collective-permute-done | bytes 294944 | tf_op jit(solution)/shard_map/ppermute | solution.py:14
  74.2 9.2 %collective-permute-done.4 = bf16[128,1152]{1,0:T(8,128)(2,1)S(1)} collective-permute-done((bf16[128,1152]{1,0:T(8,128)(2,1)S(1)}, bf16[128,1152]{1,0:T(8,128)(2,1)S(1)}, u32[]{:S(2)}, u32[]{:S(2)}) %collective-permute-start.4) | collective-permute-done | bytes 294944 | tf_op jit(solution)/shard_map/ppermute | solution.py:14
  85.3 50.3 %all-gather.3.cloned.1.call-done = bf16[512,1,1728]{2,1,0:T(2,128)(2,1)} async-done(((bf16[1,1,1728]{2,1,0:T(2,128)(2,1)}), bf16[512,1,1728]{2,1,0:T(2,128)(2,1)}) %all-gather.3.cloned.1.call-update) | async-done | bytes 1769488 | tf_op jit(solution)/shard_map/all_gather | solution.py:43
  135.6 11.4 %reduce = bf16[512,1728]{1,0:T(8,128)(2,1)S(1)} reduce(bf16[512,1,1728]{2,1,0:T(2,128)(2,1)} %all-gather.3.cloned.1.call-done, bf16[]{:T(256)} %constant.18), dimensions={1}, to_apply=%all-gather.reduce_sub_computation | reduce | bytes 3538946 | tf_op jit(solution)/shard_map/all_gather | solution.py:43
  147.1 3.7 reshape.27
  150.8 2.0 multiply_reduce_fusion.1
  153.5 2.3 collective-permute-start.6
  157.6 11.4 %collective-permute-done.6 = f32[128,1152]{1,0:T(8,128)S(1)} collective-permute-done((f32[128,1152]{1,0:T(8,128)S(1)}, f32[128,1152]{1,0:T(8,128)S(1)}, u32[]{:S(2)}, u32[]{:S(2)}) %collective-permute-start.6) | collective-permute-done | bytes 589856 | tf_op jit(solution)/shard_map/ppermute | solution.py:14
  172.0 12.7 %collective-permute-done.7 = f32[128,1152]{1,0:T(8,128)S(1)} collective-permute-done((f32[128,1152]{1,0:T(8,128)S(1)}, f32[128,1152]{1,0:T(8,128)S(1)}, u32[]{:S(2)}, u32[]{:S(2)}) %collective-permute-start.7) | collective-permute-done | bytes 589856 | tf_op jit(solution)/shard_map/ppermute | solution.py:14
  184.8 1.9 collective-permute-start.8
  189.5 10.7 %collective-permute-done.8 = f32[128,1152]{1,0:T(8,128)S(1)} collective-permute-done((f32[128,1152]{1,0:T(8,128)S(1)}, f32[128,1152]{1,0:T(8,128)S(1)}, u32[]{:S(2)}, u32[]{:S(2)}) %collective-permute-start.8) | collective-permute-done | bytes 589856 | tf_op jit(solution)/shard_map/ppermute | solution.py:14
  200.2 1.9 collective-permute-start.9
  202.2 2.5 convolution_bitcast_fusion
  204.7 5.2 %copy.10 = f32[768,1152]{1,0:T(8,128)} copy(f32[768,1152]{0,1:T(8,128)} %convolution_bitcast_fusion) | data formatting | bytes 7077888 | tf_op jit(solution)/shard_map/dot_general | solution.py:76
  209.9 5.5 %reshape.28 = f32[512,1728]{1,0:T(8,128)} reshape(f32[768,1152]{1,0:T(8,128)} %copy.10) | data formatting | bytes 7077888 | tf_op jit(solution)/shard_map/reshape | solution.py:79
  217.0 1.9 collective-permute-start.10
  219.2 13.4 %collective-permute-done.10 = f32[128,1152]{1,0:T(8,128)} collective-permute-done((f32[128,1152]{1,0:T(8,128)S(1)}, f32[128,1152]{1,0:T(8,128)}, u32[]{:S(2)}, u32[]{:S(2)}) %collective-permute-start.10) | collective-permute-done | bytes 589856 | tf_op jit(solution)/shard_map/ppermute | solution.py:14
  233.8 2.1 collective-permute-start.11
  237.2 259.7 %all-reduce.3.cloned.1.call-done = f32[512,1728]{1,0:T(8,128)} async-done(((f32[512,1728]{1,0:T(8,128)}), f32[512,1728]{1,0:T(8,128)}) %all-reduce.3.cloned.1.call-update) | async-done | bytes 3538960
  (67 shorter events, 25.8 us)
Async XLA Ops:
  7.2 143.6 %copy-start = (bf16[128,768]{1,0:T(8,128)(2,1)S(1)}, bf16[128,768]{1,0:T(8,128)(2,1)}, u32[]{:S(2)}) copy-start(bf16[128,768]{1,0:T(8,128)(2,1)} %param.6) | copy-start | bytes 589828
  7.2 128.4 %all-gather.3.cloned.1.call-start = ((), (), s32[]{:S(2)}) async-start(), calls=%async_computation | async-start | bytes 3677184 | tf_op jit(solution)/shard_map/all_gather | solution.py:43
  7.9 489.0 %all-reduce.3.cloned.1.call-start = ((), (), s32[]{:S(2)}) async-start(), calls=%async_computation.1 | async-start | bytes 7340032
  10.2 23.8 %collective-permute-start = (bf16[128,1152]{1,0:T(8,128)(2,1)S(1)}, bf16[128,1152]{1,0:T(8,128)(2,1)S(1)}, u32[]{:S(2)}, u32[]{:S(2)}) collective-permute-start(bf16[128,1152]{1,0:T(8,128)(2,1)S(1)} %fusion.47), channel_id=1, source_target_pairs={{0,509},{1,510},{2,511},{3,0},{4,1},{5,2},{6,3},{7,4},{8,5},{9,6},... | collective-permute-start | bytes 884744 | tf_op jit(solution)/shard_map/ppermute | solution.py:14
  34.0 12.3 %collective-permute-start.1 = (bf16[128,1152]{1,0:T(8,128)(2,1)S(1)}, bf16[128,1152]{1,0:T(8,128)(2,1)S(1)}, u32[]{:S(2)}, u32[]{:S(2)}) collective-permute-start(bf16[128,1152]{1,0:T(8,128)(2,1)S(1)} %collective-permute-done), channel_id=1, source_target_pairs={{0,1},{1,2},{2,3},{3,4},{4,5},{5,6},{6,7},{7,8},{8,9},{9,10},{10,1... | collective-permute-start | bytes 884744 | tf_op jit(solution)/shard_map/ppermute | solution.py:14
  46.3 12.3 %collective-permute-start.2 = (bf16[128,1152]{1,0:T(8,128)(2,1)S(1)}, bf16[128,1152]{1,0:T(8,128)(2,1)S(1)}, u32[]{:S(2)}, u32[]{:S(2)}) collective-permute-start(bf16[128,1152]{1,0:T(8,128)(2,1)S(1)} %collective-permute-done.1), channel_id=1, source_target_pairs={{0,1},{1,2},{2,3},{3,4},{4,5},{5,6},{6,7},{7,8},{8,9},{9,10},{10,1... | collective-permute-start | bytes 884744 | tf_op jit(solution)/shard_map/ppermute | solution.py:14
  58.6 88.5 %copy-start.10 = (bf16[128,1152]{1,0:T(8,128)(2,1)}, bf16[128,1152]{1,0:T(8,128)(2,1)S(1)}, u32[]{:S(2)}) copy-start(bf16[128,1152]{1,0:T(8,128)(2,1)S(1)} %collective-permute-done.2) | copy-start | bytes 884740
  58.6 12.4 %collective-permute-start.3 = (bf16[128,1152]{1,0:T(8,128)(2,1)S(1)}, bf16[128,1152]{1,0:T(8,128)(2,1)S(1)}, u32[]{:S(2)}, u32[]{:S(2)}) collective-permute-start(bf16[128,1152]{1,0:T(8,128)(2,1)S(1)} %collective-permute-done.2), channel_id=1, source_target_pairs={{0,1},{1,2},{2,3},{3,4},{4,5},{5,6},{6,7},{7,8},{8,9},{9,10},{10,1... | collective-permute-start | bytes 884744 | tf_op jit(solution)/shard_map/ppermute | solution.py:14
  70.9 76.1 %copy-start.6 = (bf16[128,1152]{1,0:T(8,128)(2,1)}, bf16[128,1152]{1,0:T(8,128)(2,1)S(1)}, u32[]{:S(2)}) copy-start(bf16[128,1152]{1,0:T(8,128)(2,1)S(1)} %collective-permute-done.3) | copy-start | bytes 884740
  70.9 12.4 %collective-permute-start.4 = (bf16[128,1152]{1,0:T(8,128)(2,1)S(1)}, bf16[128,1152]{1,0:T(8,128)(2,1)S(1)}, u32[]{:S(2)}, u32[]{:S(2)}) collective-permute-start(bf16[128,1152]{1,0:T(8,128)(2,1)S(1)} %collective-permute-done.3), channel_id=1, source_target_pairs={{0,1},{1,2},{2,3},{3,4},{4,5},{5,6},{6,7},{7,8},{8,9},{9,10},{10,1... | collective-permute-start | bytes 884744 | tf_op jit(solution)/shard_map/ppermute | solution.py:14
  83.4 103.3 %collective-permute-start.5 = (bf16[128,1152]{1,0:T(8,128)(2,1)S(1)}, bf16[128,1152]{1,0:T(8,128)(2,1)}, u32[]{:S(2)}, u32[]{:S(2)}) collective-permute-start(bf16[128,1152]{1,0:T(8,128)(2,1)S(1)} %collective-permute-done.4), channel_id=1, source_target_pairs={{0,1},{1,2},{2,3},{3,4},{4,5},{5,6},{6,7},{7,8},{8,9},{9,10},{10,1... | collective-permute-start | bytes 884744 | tf_op jit(solution)/shard_map/ppermute | solution.py:14
  147.1 3.7 copy-start.5
  153.2 3.4 copy-start.9
  153.4 3.4 copy-start.7
  153.5 15.6 %collective-permute-start.6 = (f32[128,1152]{1,0:T(8,128)S(1)}, f32[128,1152]{1,0:T(8,128)S(1)}, u32[]{:S(2)}, u32[]{:S(2)}) collective-permute-start(f32[128,1152]{1,0:T(8,128)S(1)} %fusion.50), channel_id=1, source_target_pairs={{0,1},{1,2},{2,3},{3,4},{4,5},{5,6},{6,7},{7,8},{8,9},{9,10},{10,1... | collective-permute-start | bytes 1769480 | tf_op jit(solution)/shard_map/ppermute | solution.py:14
  169.3 15.4 %collective-permute-start.7 = (f32[128,1152]{1,0:T(8,128)S(1)}, f32[128,1152]{1,0:T(8,128)S(1)}, u32[]{:S(2)}, u32[]{:S(2)}) collective-permute-start(f32[128,1152]{1,0:T(8,128)S(1)} %convolution_add_fusion.1), channel_id=1, source_target_pairs={{0,1},{1,2},{2,3},{3,4},{4,5},{5,6},{6,7},{7,8},{8,9},{9,10},{10,1... | collective-permute-start | bytes 1769480 | tf_op jit(solution)/shard_map/ppermute | solution.py:14
  184.8 15.4 %collective-permute-start.8 = (f32[128,1152]{1,0:T(8,128)S(1)}, f32[128,1152]{1,0:T(8,128)S(1)}, u32[]{:S(2)}, u32[]{:S(2)}) collective-permute-start(f32[128,1152]{1,0:T(8,128)S(1)} %add.118), channel_id=1, source_target_pairs={{0,1},{1,2},{2,3},{3,4},{4,5},{5,6},{6,7},{7,8},{8,9},{9,10},{10,1... | collective-permute-start | bytes 1769480 | tf_op jit(solution)/shard_map/ppermute | solution.py:14
  189.5 12.7 %copy-start.3 = (f32[128,1152]{1,0:T(8,128)}, f32[128,1152]{1,0:T(8,128)S(1)}, u32[]{:S(2)}) copy-start(f32[128,1152]{1,0:T(8,128)S(1)} %get-tuple-element.6) | copy-start | bytes 1769476
  200.2 15.5 %collective-permute-start.9 = (f32[128,1152]{1,0:T(8,128)S(1)}, f32[128,1152]{1,0:T(8,128)}, u32[]{:S(2)}, u32[]{:S(2)}) collective-permute-start(f32[128,1152]{1,0:T(8,128)S(1)} %add.119), channel_id=1, source_target_pairs={{0,1},{1,2},{2,3},{3,4},{4,5},{5,6},{6,7},{7,8},{8,9},{9,10},{10,1... | collective-permute-start | bytes 1769480 | tf_op jit(solution)/shard_map/ppermute | solution.py:14
  215.7 20.2 %copy-start.1 = (bf16[768,1152]{1,0:T(8,128)(2,1)S(1)}, bf16[768,1152]{1,0:T(8,128)(2,1)}, u32[]{:S(2)}) copy-start(bf16[768,1152]{1,0:T(8,128)(2,1)} %reshape.27) | copy-start | bytes 5308420
  217.0 15.6 %collective-permute-start.10 = (f32[128,1152]{1,0:T(8,128)S(1)}, f32[128,1152]{1,0:T(8,128)}, u32[]{:S(2)}, u32[]{:S(2)}) collective-permute-start(f32[128,1152]{1,0:T(8,128)S(1)} %add.120), channel_id=1, source_target_pairs={{0,1},{1,2},{2,3},{3,4},{4,5},{5,6},{6,7},{7,8},{8,9},{9,10},{10,1... | collective-permute-start | bytes 1769480 | tf_op jit(solution)/shard_map/ppermute | solution.py:14
  218.9 16.9 %copy-start.4 = (f32[128,1152]{1,0:T(8,128)S(1)}, f32[128,1152]{1,0:T(8,128)}, u32[]{:S(2)}) copy-start(f32[128,1152]{1,0:T(8,128)} %copy-done.3) | copy-start | bytes 1769476
  233.8 264.6 %copy-start.2 = (bf16[128,1152]{1,0:T(8,128)(2,1)S(1)}, bf16[128,1152]{1,0:T(8,128)(2,1)}, u32[]{:S(2)}) copy-start(bf16[128,1152]{1,0:T(8,128)(2,1)} %param.9) | copy-start | bytes 884740
  233.8 264.6 %collective-permute-start.11 = (bf16[128,1152]{1,0:T(8,128)(2,1)S(1)}, bf16[128,1152]{1,0:T(8,128)(2,1)S(1)}, u32[]{:S(2)}, u32[]{:S(2)}) collective-permute-start(bf16[128,1152]{1,0:T(8,128)(2,1)S(1)} %add_convert_fusion), channel_id=1, source_target_pairs={{0,510},{1,511},{2,0},{3,1},{4,2},{5,3},{6,4},{7,5},{8,6},{9,7},{1... | collective-permute-start | bytes 884744 | tf_op jit(solution)/shard_map/ppermute | solution.py:14
  (2 other events, 4.9 us)
Sparse Core Ops, SparseCore 0:
  12.2 123.3 all-gather.2
  215.5 281.3 all-reduce.2
where the time goes:
time: 510 us; the launch traced here: 506 us
  waiting for transfers between devices  410 us (80%)
  starting transfers between devices  35.3 us (7%)
  other arithmetic  17.5 us (3%)
  local copies, waits for them, and re-layouts  15.9 us (3%)
  between operations  15.8 us (3%)
  matrix products  12.3 us (2%)
    unnamed x3, waiting for transfers between devices  260 us
    ppermute x12, waiting for transfers between devices, shifted(): return lax.ppermute(value, axis, pairs)  99 us
    all_gather x1, waiting for transfers between devices, body(): lax.all_gather(head_weight, 'dp', axis=0, tiled=True).reshape(KW, D)  50.3 us
    ppermute x12, starting transfers between devices, shifted(): return lax.ppermute(value, axis, pairs)  35.2 us
    all_gather x1, other arithmetic, body(): lax.all_gather(head_weight, 'dp', axis=0, tiled=True).reshape(KW, D)  11.4 us
  transfers between devices with their start and end apart: 14, of which 12 were waited for; matrix products, arithmetic and copies ran while one was open for 9% of the time, Pallas kernels for 0%

commit v1 on v0

v1 whole, which is shorter than its diff:
```python
import functools

import jax
import jax.numpy as jnp
from jax import lax
from jax.experimental import pallas as pl
from jax.experimental.pallas import tpu as pltpu
from jax.sharding import PartitionSpec as P

D = 1152
GROUP = 1728
LANES = 128
TILES = 14
HALF = 896
WINDOW = 6
X, Y, Z = 4, 8, 8
EPS = 1e-06
F32 = jnp.float32
BF16 = jnp.bfloat16
MESH = pl.DeviceIdType.MESH


def dot(a, b):
    return jnp.dot(a, b, preferred_element_type=F32)


def dot_t(a, b):
    return lax.dot_general(a, b, (((1,), (1,)), ((), ())), preferred_element_type=F32)


def ring_order(n):
    return sorted(range(1, n), key=lambda d: (min(d, n - d), d))


def kernel(
    dims,
    pooled_ref, other_ref, shard_ref, text_ref, scale_ref, bias_ref,
    pooled_grad_ref, text_grad_ref, weight_grad_ref,
    fold, column, wbuf, bpart, tbuf, ibuf, pool2, grad2, qmat, pat, pbt,
    gsend, gown, grecv, ysend, yown, yrecv, zsend, zrecv,
    col_s, col_r, wy_s, wy_r, wx_s, wx_r, wsib_s, wsib_r,
    text_s, text_r, img_s, img_r, pair_s, pair_r,
    gx_s, gx_r, gy_s, gy_r, gz_s, gz_r,
):
    nx, ny, nz = dims
    count = nx * ny * nz * 2
    rows = 2 * nz
    span = ny * rows
    tok = pooled_ref.shape[0]
    kw = pooled_ref.shape[1]
    chips = count // 2

    me = lax.axis_index("dp")
    c = me % 2
    z = (me // 2) % nz
    y = (me // (2 * nz)) % ny
    x = me // (2 * nz * ny)
    sib = me + 1 - 2 * c

    def device(xx, yy, zz, cc):
        return ((xx * ny + yy) * nz + zz) * 2 + cc

    def ring(step):
        return (me + step + count) % count

    def send(src, dst, ssem, rsem, to):
        pltpu.make_async_remote_copy(
            src_ref=src, dst_ref=dst, send_sem=ssem, recv_sem=rsem, device_id=(to,), device_id_type=MESH
        ).start()

    def wait(ref, sem):
        pltpu.make_async_copy(ref, ref, sem).wait()

    ydist = ring_order(ny)
    xdist = ring_order(nx)

    barrier = pltpu.get_barrier_semaphore()

    def hello(to):
        pl.semaphore_signal(barrier, inc=1, device_id=(to,), device_id_type=MESH)

    def hello_column(i, carry):
        hello(device(x, y, (z + i // 2) % nz, (c + i) % 2))
        return carry

    lax.fori_loop(1, 2 * nz, hello_column, 0)
    for d in ydist:
        hello(device(x, (y + d) % ny, z, c))
    for d in xdist:
        hello(device((x + d) % nx, y, z, c))
    for d in (-3, -2, -1, 1, 2, 3):
        hello(ring(d))

    piece = shard_ref[...].astype(F32)
    fold[...] = jnp.zeros_like(fold)
    for r in range(TILES - 1):
        fold[r : r + 1, :] = piece[:, r * LANES : (r + 1) * LANES]
    fold[TILES - 1 : TILES, : LANES // 2] = piece[:, (TILES - 1) * LANES :]
    slot = c * nz + z
    column[slot] = fold[...].astype(BF16)

    text = text_ref[...].astype(F32)
    text_inv = 1.0 / jnp.sqrt(jnp.sum(text * text, axis=1, keepdims=True) + EPS)
    tbuf[2] = (text * text_inv).astype(BF16)
    pool2[c] = pooled_ref[...]

    pl.semaphore_wait(barrier, 2 * nz - 1 + len(ydist) + len(xdist) + 6)

    def send_column(i, carry):
        to = device(x, y, (z + i // 2) % nz, (c + i) % 2)
        send(column.at[slot], column.at[slot], col_s.at[i], col_r.at[slot], to)
        return carry

    lax.fori_loop(1, 2 * nz, send_column, 0)

    send(tbuf.at[2], tbuf.at[4], text_s.at[0], text_r.at[4], ring(-2))
    far = jnp.where(c == 0, -3, 1)
    send(tbuf.at[2], tbuf.at[2 - far], text_s.at[1], text_r.at[2 - far], ring(far))
    send(tbuf.at[2], tbuf.at[0], text_s.at[2], text_r.at[0], ring(2))
    to_sib = 1 + 2 * c
    send(tbuf.at[2], tbuf.at[to_sib], text_s.at[3], text_r.at[to_sib], sib)
    send(pool2.at[c], pool2.at[c], pair_s.at[0], pair_r.at[0], sib)

    j = lax.broadcasted_iota(jnp.int32, (kw, count), 0)
    a = lax.broadcasted_iota(jnp.int32, (kw, count), 1)
    pick_a = j == 3 * ((a // rows) * nz + a % nz) + 2 * ((a // nz) % 2)
    pick_a = pick_a.astype(F32).astype(BF16)
    jb = lax.broadcasted_iota(jnp.int32, (kw, chips), 0)
    kb = lax.broadcasted_iota(jnp.int32, (kw, chips), 1)
    pick_b = (jb == 3 * kb + 1).astype(F32).astype(BF16)
    own_pooled = pooled_ref[...]
    qmat[:, :count] = dot(own_pooled, pick_a).astype(BF16)
    qmat[:, count:] = dot(own_pooled, pick_b).astype(BF16)

    def wait_column(i, carry):
        other = ((c + i) % 2) * nz + (z + i // 2) % nz
        wait(column.at[other], col_r.at[other])
        return carry

    lax.fori_loop(1, 2 * nz, wait_column, 0)
    turn_a = lax.broadcasted_iota(jnp.int32, (16 * rows, 16 * rows), 0)
    turn_b = lax.broadcasted_iota(jnp.int32, (16 * rows, 16 * rows), 1)
    turn = ((turn_a // rows == turn_b % 16) & (turn_a % rows == turn_b // 16)).astype(F32).astype(BF16)
    turned = dot(turn, column[...].reshape(16 * rows, LANES))
    even = [turned[r * rows : r * rows + nz] for r in range(TILES)]
    odd = [pltpu.roll(turned[r * rows + nz : (r + 1) * rows], LANES // 2, 1) for r in range(TILES)]
    low = lax.broadcasted_iota(jnp.int32, (nz, LANES), 1) < LANES // 2
    tiles = [jnp.concatenate([even[b], jnp.where(low, odd[4 + b], odd[5 + b])], axis=0) for b in range(9)]
    middle = even[9:13] + [jnp.where(low, even[13], odd[0])]
    middle += [jnp.where(low, odd[b - 5], odd[b - 4]) for b in range(5, 9)] + [jnp.zeros((nz, LANES), F32)]
    tiles += [jnp.concatenate([middle[b], middle[5 + b]], axis=0) for b in range(5)]
    here = pl.multiple_of((x * ny + y) * rows, rows)
    for t in range(7):
        wbuf[c, pl.ds(here, rows), t * LANES : (t + 1) * LANES] = jnp.where(
            c == 0, tiles[t], tiles[7 + t]
        ).astype(BF16)

    def block(xx, yy):
        return wbuf.at[c, pl.ds(pl.multiple_of((xx * ny + yy) * rows, rows), rows), :]

    def share_x(yy, k):
        for d in xdist:
            send(block(x, yy), block(x, yy), wx_s.at[k, d], wx_r.at[x, yy], device((x + d) % nx, y, z, c))

    for d in ydist:
        send(block(x, y), block(x, y), wy_s.at[d], wy_r.at[y], device(x, (y + d) % ny, z, c))
    share_x(y, 0)
    for d in ydist:
        yy = (y + d) % ny
        wait(block(x, yy), wy_r.at[yy])
        share_x(yy, d)

    def whole(core, xx):
        return wbuf.at[core, pl.ds(pl.multiple_of(xx * span, span), span), :]

    send(whole(c, x), whole(c, x), wsib_s.at[0], wsib_r.at[x], sib)

    wait(pool2.at[1 - c], pair_r.at[0])
    jt = lax.broadcasted_iota(jnp.int32, (chips, kw), 1)
    kt = lax.broadcasted_iota(jnp.int32, (chips, kw), 0)
    both = pool2[...].reshape(2 * tok, kw)
    pat[...] = dot_t((jt == 3 * kt + 2 * c).astype(F32).astype(BF16), both).astype(BF16)
    pbt[...] = dot_t((jt == 3 * kt + 1).astype(F32).astype(BF16), both).astype(BF16)

    wait(tbuf.at[4], text_r.at[4])
    pass_to = 3 + 2 * c
    send(tbuf.at[4], tbuf.at[pass_to], text_s.at[4], text_r.at[pass_to], sib)

    for d in xdist:
        xx = (x + d) % nx
        for yy in range(ny):
            wait(block(xx, yy), wx_r.at[xx, yy])
        send(whole(c, xx), whole(c, xx), wsib_s.at[d], wsib_r.at[xx], sib)
    for d in [0] + xdist:
        xx = (x + d) % nx
        wait(whole(1 - c, xx), wsib_r.at[xx])

    packed = wbuf[1, :, 2 * LANES :].astype(F32).reshape(nx * ny, rows, 5 * LANES)
    bpart[:, : 5 * LANES] = packed[:, :nz].reshape(chips, 5 * LANES).astype(BF16)
    bpart[:, 5 * LANES :] = packed[:, nz:, : 4 * LANES].reshape(chips, 4 * LANES).astype(BF16)

    qa, qb = qmat[:, :count], qmat[:, count:]
    image = jnp.concatenate(
        [
            dot(qa, wbuf[0]) + dot(qb, bpart[:, :HALF]),
            dot(qa, wbuf[1, :, : 2 * LANES]) + dot(qb, bpart[:, HALF:]),
        ],
        axis=1,
    ) + other_ref[...].astype(F32)
    image_inv = 1.0 / jnp.sqrt(jnp.sum(image * image, axis=1, keepdims=True) + EPS)
    image_unit = image * image_inv
    ibuf[3] = image_unit.astype(BF16)

    send(ibuf.at[3], ibuf.at[1], img_s.at[0], img_r.at[1], ring(2))
    afar = jnp.where(c == 1, 3, -1)
    send(ibuf.at[3], ibuf.at[3 - afar], img_s.at[1], img_r.at[3 - afar], ring(afar))
    send(ibuf.at[3], ibuf.at[5], img_s.at[2], img_r.at[5], ring(-2))
    img_sib = 2 + 2 * c
    send(ibuf.at[3], ibuf.at[img_sib], img_s.at[3], img_r.at[img_sib], sib)

    temper = jnp.exp(jnp.full((1, 1), scale_ref[0], F32))
    bias = bias_ref[0]
    row = lax.broadcasted_iota(jnp.int32, (tok, WINDOW * tok), 0)
    col = lax.broadcasted_iota(jnp.int32, (tok, WINDOW * tok), 1)

    def pairs(unit, blocks, own):
        logits = temper * dot_t(unit, blocks) + bias
        sign = jnp.where(col == row + own * tok, -1.0, 1.0)
        coef = (temper * sign / (1.0 + jnp.exp(-sign * logits))).astype(BF16)
        return dot(coef, blocks)

    for k in (0, 1, 3, 5):
        wait(tbuf.at[k], text_r.at[k])
    emb_grad = pairs(ibuf[3], tbuf[...].reshape(WINDOW * tok, D), 2)
    image_grad = (
        (emb_grad - image_unit * jnp.sum(image_unit * emb_grad, axis=1, keepdims=True)) * image_inv
    ).astype(BF16)
    grad2[c] = image_grad
    send(grad2.at[c], grad2.at[c], pair_s.at[1], pair_r.at[1], sib)

    wait(grad2.at[1 - c], pair_r.at[1])
    grads = grad2[...].reshape(2 * tok, D)
    side = jnp.where(c == 0, grads[:, : 5 * LANES], grads[:, 4 * LANES :])

    def term(xx):
        at = pl.ds(pl.multiple_of(xx * ny * nz, ny * nz), ny * nz)
        full = dot(pat[at, :], grads)
        tail = dot(pbt[at, :], side)
        top = full[:, :HALF].reshape(ny, nz, HALF)
        end = jnp.concatenate([full[:, HALF:], tail], axis=1).reshape(ny, nz, HALF)
        return jnp.concatenate([top, end], axis=1)

    for d in xdist[::-1]:
        xx = (x + d) % nx
        gsend[d] = term(xx).astype(BF16)
        for e in ydist + [0]:
            yy = (y + e) % ny
            send(gsend.at[d, yy], grecv.at[x, yy], gx_s.at[d, yy], gx_r.at[x, yy], device(xx, y, z, c))
    gown[...] = term(x)

    wait(ibuf.at[1], img_r.at[1])
    img_pass = 2 * c
    send(ibuf.at[1], ibuf.at[img_pass], img_s.at[4], img_r.at[img_pass], sib)

    def sum_x(yy):
        total = gown[yy]
        for d in xdist:
            xx = (x + d) % nx
            wait(grecv.at[xx, yy], gx_r.at[xx, yy])
            total += grecv[xx, yy].astype(F32)
        return total

    for e in ydist:
        yy = (y + e) % ny
        ysend[yy] = sum_x(yy).astype(BF16)
        send(ysend.at[yy], yrecv.at[y], gy_s.at[yy], gy_r.at[y], device(x, yy, z, c))
    yown[...] = sum_x(y)

    own_grad = grad2[c]
    to_a = dot_t(own_grad[:, :HALF], wbuf[0]) + dot_t(own_grad[:, HALF:], wbuf[1, :, : 2 * LANES])
    to_b = dot_t(own_grad, bpart[...])
    pooled_grad_ref[...] = (dot_t(to_a.astype(BF16), pick_a) + dot_t(to_b.astype(BF16), pick_b)).astype(BF16)

    total = yown[...]
    for e in ydist:
        yy = (y + e) % ny
        wait(yrecv.at[yy], gy_r.at[yy])
        total += yrecv[yy].astype(F32)
    zsend[...] = jnp.zeros_like(zsend)
    for t in range(TILES):
        part = total[:nz] if t < 7 else total[nz:]
        zsend[pl.ds(t, nz, stride=16), :] = part[:, (t % 7) * LANES : (t % 7 + 1) * LANES]

    def zrow(zz):
        return zsend.at[pl.ds(pl.multiple_of(zz * 16, 16), 16), :]

    for e in ring_order(nz):
        zz = (z + e) % nz
        send(zrow(zz), zrecv.at[z], gz_s.at[zz], gz_r.at[z], device(x, y, zz, c))

    for k in (0, 2, 4, 5):
        wait(ibuf.at[k], img_r.at[k])
    text_emb_grad = pairs(tbuf[2], ibuf[...].reshape(WINDOW * tok, D), 3)
    text_again = text_ref[...].astype(F32)
    again_inv = 1.0 / jnp.sqrt(jnp.sum(text_again * text_again, axis=1, keepdims=True) + EPS)
    text_unit = text_again * again_inv
    text_grad_ref[...] = (
        text_emb_grad - text_unit * jnp.sum(text_unit * text_emb_grad, axis=1, keepdims=True)
    ) * again_inv

    summed = zsend[pl.ds(pl.multiple_of(z * 16, 16), 16), :]
    for e in ring_order(nz):
        zz = (z + e) % nz
        wait(zrecv.at[zz], gz_r.at[zz])
        summed += zrecv[zz]
    weight_grad_ref[...] = summed

    def sent_column(i, carry):
        wait(column.at[slot], col_s.at[i])
        return carry

    lax.fori_loop(1, 2 * nz, sent_column, 0)
    for k in range(5):
        wait(tbuf.at[2], text_s.at[k])
        wait(ibuf.at[3], img_s.at[k])
    wait(pool2.at[c], pair_s.at[0])
    wait(grad2.at[c], pair_s.at[1])
    for d in ydist:
        wait(block(x, y), wy_s.at[d])
    for d in xdist:
        for k in range(ny):
            wait(block(x, y), wx_s.at[k, d])
            wait(gsend.at[d, k], gx_s.at[d, k])
    for d in [0] + xdist:
        wait(whole(c, x), wsib_s.at[d])
    for e in ydist:
        yy = (y + e) % ny
        wait(ysend.at[yy], gy_s.at[yy])
    for e in ring_order(nz):
        zz = (z + e) % nz
        wait(zrow(zz), gz_s.at[zz])


def body(dims, pooled, other_part, head_weight, text, logit_scale, logit_bias):
    nx, ny, nz = dims
    count = 2 * nx * ny * nz
    tok, kw = pooled.shape
    rows = 2 * nz
    dma = lambda *shape: pltpu.SemaphoreType.DMA(shape)
    vmem = pl.BlockSpec(memory_space=pltpu.VMEM)
    smem = pl.BlockSpec(memory_space=pltpu.SMEM)
    pooled_grad, text_grad, total = pl.pallas_call(
        functools.partial(kernel, dims),
        out_shape=(
            jax.ShapeDtypeStruct((tok, kw), BF16),
            jax.ShapeDtypeStruct((tok, D), F32),
            jax.ShapeDtypeStruct((16, LANES), F32),
        ),
        in_specs=[vmem, vmem, vmem, vmem, smem, smem],
        out_specs=(vmem, vmem, vmem),
        scratch_shapes=[
            pltpu.VMEM((16, LANES), F32),
            pltpu.VMEM((rows, 16, LANES), BF16),
            pltpu.VMEM((2, count, HALF), BF16),
            pltpu.VMEM((count // 2, D), BF16),
            pltpu.VMEM((WINDOW, tok, D), BF16),
            pltpu.VMEM((WINDOW, tok, D), BF16),
            pltpu.VMEM((2, tok, kw), BF16),
            pltpu.VMEM((2, tok, D), BF16),
            pltpu.VMEM((tok, kw), BF16),
            pltpu.VMEM((count // 2, 2 * tok), BF16),
            pltpu.VMEM((count // 2, 2 * tok), BF16),
            pltpu.VMEM((nx, ny, rows, HALF), BF16),
            pltpu.VMEM((ny, rows, HALF), F32),
            pltpu.VMEM((nx, ny, rows, HALF), BF16),
            pltpu.VMEM((ny, rows, HALF), BF16),
            pltpu.VMEM((rows, HALF), F32),
            pltpu.VMEM((ny, rows, HALF), BF16),
            pltpu.VMEM((nz * 16, LANES), F32),
            pltpu.VMEM((nz, 16, LANES), F32),
            dma(rows), dma(rows),
            dma(ny), dma(ny),
            dma(ny, nx), dma(nx, ny),
            dma(nx), dma(nx),
            dma(5), dma(WINDOW),
            dma(5), dma(WINDOW),
            dma(2), dma(2),
            dma(nx, ny), dma(nx, ny),
            dma(ny), dma(ny),
            dma(nz), dma(nz),
        ],
        compiler_params=pltpu.CompilerParams(
            collective_id=0, has_side_effects=True, vmem_limit_bytes=48 * 1024 * 1024
        ),
    )(pooled, other_part, head_weight, text, logit_scale, logit_bias)
    flat = total[:TILES].reshape(1, TILES * LANES)
    first = flat[:, :GROUP]
    second = jnp.concatenate([flat[:, D + 64 :], flat[:, :D]], axis=1)
    weight_grad = jnp.where(lax.axis_index("dp") % 2 == 0, first, second)
    return pooled_grad, text_grad, weight_grad


def solution(mesh, dims=(X, Y, Z)):
    return jax.shard_map(
        functools.partial(body, dims),
        mesh=mesh,
        in_specs=(P("dp", None), P("dp", None), P("dp", None), P("dp", None), P(), P()),
        out_specs=(P("dp", None), P("dp", None), P("dp", None)),
        check_vma=False,
    )
```

time: 510 us -> 81.6 us (0.16)
  waiting for transfers between devices: 410 us -> 0 us
  Pallas kernels: 0 us -> 73.2 us
  starting transfers between devices: 35.3 us -> 0 us
  other arithmetic: 17.5 us -> 0.68 us
  between operations: 15.8 us -> 1.99 us
  matrix products: 12.3 us -> 0 us
  local copies, waits for them, and re-layouts: 15.9 us -> 4.42 us
    unnamed x3 -> x0, waiting for transfers between devices: 260 us -> none
    ppermute x12 -> x0, waiting for transfers between devices: 99 us -> none  [shifted(): return lax.ppermute(value, axis, pairs)]
    pallas_call x0 -> x1, Pallas kernels: none -> 73.2 us  [body(): pl.pallas_call(functools.partial(kernel, dims), out_shape=(jax.ShapeDtype...]
    all_gather x1 -> x0, waiting for transfers between devices: 50.3 us -> none  [body(): lax.all_gather(head_weight, 'dp', axis=0, tiled=True).reshape(KW, D)]
    ppermute x12 -> x0, starting transfers between devices: 35.2 us -> none  [shifted(): return lax.ppermute(value, axis, pairs)]
    dot_general x21 -> x0, matrix products: 12.3 us -> none  [the longest x6 2.56 us: tile_coef(): lax.dot_general(image_emb, block, (((1,), (1,)), ((), ())), preferred_ele...]
    all_gather x1 -> x0, other arithmetic: 11.4 us -> none  [body(): lax.all_gather(head_weight, 'dp', axis=0, tiled=True).reshape(KW, D)]
    reshape x2 -> x0, local copies, waits for them, and re-layouts: 9.22 us -> none  [the longest x1 5.53 us: body(): weight_term = weight_term.reshape(lax.axis_size('dp'), -1)]
  transfers between devices with their start and end apart: 14 -> 0, of which waited for: 12 -> 0; matrix products, arithmetic and copies ran while one was open for 9% -> 0% of each run, Pallas kernels for 0% -> 0%
where the time goes in v1:
time: 81.6 us; the launch traced here: 80.3 us
  Pallas kernels  73.2 us (90%)
  local copies, waits for them, and re-layouts  4.42 us (5%)
  between operations  1.99 us (2%)
    pallas_call x1, Pallas kernels, body(): pl.pallas_call(functools.partial(kernel, dims), out_shape=(jax.ShapeDtype...  73.2 us
    unnamed x12, local copies, waits for them, and re-layouts  4.35 us

profile of v1, /device:TPU:6, one launch (start us, length us, event | category | flops | bytes accessed | tf_op | source)
XLA Modules:
  0.0 80.3 jit_solution(10527603444953388706)
XLA Ops:
  0.6 0.0 copy-start.3
  1.9 0.0 copy-done.3
  2.0 0.0 copy-start
  2.0 1.0 %copy-done = bf16[128,1152]{1,0:T(8,128)(2,1)S(1)} copy-done((bf16[128,1152]{1,0:T(8,128)(2,1)S(1)}, bf16[128,1152]{1,0:T(8,128)(2,1)}, u32[]{:S(2)}) %copy-start) | copy-done | bytes 294936
  2.9 0.0 copy-start.1
  2.9 1.0 %copy-done.1 = bf16[128,1152]{1,0:T(8,128)(2,1)S(1)} copy-done((bf16[128,1152]{1,0:T(8,128)(2,1)S(1)}, bf16[128,1152]{1,0:T(8,128)(2,1)}, u32[]{:S(2)}) %copy-start.1) | copy-done | bytes 294936
  3.9 0.0 copy-start.2
  3.9 0.9 %copy-done.2 = bf16[128,768]{1,0:T(8,128)(2,1)S(1)} copy-done((bf16[128,768]{1,0:T(8,128)(2,1)S(1)}, bf16[128,768]{1,0:T(8,128)(2,1)}, u32[]{:S(2)}) %copy-start.2) | copy-done | bytes 196632
  4.8 73.2 %shard_map.85 = (bf16[128,768]{1,0:T(8,128)(2,1)S(1)}, f32[128,1152]{1,0:T(8,128)S(1)}, f32[16,128]{1,0:T(8,128)S(1)}) custom-call(bf16[128,768]{1,0:T(8,128)(2,1)S(1)} %copy-done.2, bf16[128,1152]{1,0:T(8,128)(2,1)S(1)} %copy-done, bf16[1,1728]{1,0:T(2,128)(2,1)S(1)} %copy-done.3, bf16[128,1152]{1,0:T(8,128)(2,1)S(1)} %copy-done.1, f32[1]{0:T(128)S(6)} %copy.14.scale_ref, ...), custom_call_target="tpu_custom_call" | custom-call | tf_op jit(solution)/shard_map/pallas_call | solution.py:352
  78.0 0.1 slice.17
  78.1 0.7 broadcast_select_fusion
  78.8 0.7 copy.16
  79.4 0.8 %copy.17 = f32[128,1152]{1,0:T(8,128)} copy(f32[128,1152]{1,0:T(8,128)S(1)} %get-tuple-element.13) | data formatting | bytes 1179648
  (3 shorter events, 0.0 us)
Async XLA Ops:
  0.6 1.3 %copy-start.3 = (bf16[1,1728]{1,0:T(2,128)(2,1)S(1)}, bf16[1,1728]{1,0:T(2,128)(2,1)}, u32[]{:S(2)}) copy-start(bf16[1,1728]{1,0:T(2,128)(2,1)} %shard_ref.1) | copy-start | bytes 10372
  2.0 1.0 %copy-start = (bf16[128,1152]{1,0:T(8,128)(2,1)S(1)}, bf16[128,1152]{1,0:T(8,128)(2,1)}, u32[]{:S(2)}) copy-start(bf16[128,1152]{1,0:T(8,128)(2,1)} %other_ref.1) | copy-start | bytes 884740
  2.9 1.0 %copy-start.1 = (bf16[128,1152]{1,0:T(8,128)(2,1)S(1)}, bf16[128,1152]{1,0:T(8,128)(2,1)}, u32[]{:S(2)}) copy-start(bf16[128,1152]{1,0:T(8,128)(2,1)} %text_ref.1) | copy-start | bytes 884740
  3.9 0.9 %copy-start.2 = (bf16[128,768]{1,0:T(8,128)(2,1)S(1)}, bf16[128,768]{1,0:T(8,128)(2,1)}, u32[]{:S(2)}) copy-start(bf16[128,768]{1,0:T(8,128)(2,1)} %pooled_ref.1) | copy-start | bytes 589828

commit v2 on v1

--- a/solution.py
+++ b/solution.py
@@ -15,6 +15,11 @@
 WINDOW = 6
 X, Y, Z = 4, 8, 8
 EPS = 1e-06
+LAG = 2
+BY_RIGHT = (0, 2, 4)
+DIRECT = (5, 6, 7)
+SUM_RIGHT = (3, 5)
+SUM_NONE = (0, 1, 2)
 F32 = jnp.float32
 BF16 = jnp.bfloat16
 MESH = pl.DeviceIdType.MESH
@@ -34,13 +39,14 @@
 
 def kernel(
     dims,
-    pooled_ref, other_ref, shard_ref, text_ref, scale_ref, bias_ref,
+    pooled_hbm, other_hbm, shard_hbm, text_hbm, scale_ref, bias_ref,
     pooled_grad_ref, text_grad_ref, weight_grad_ref,
+    pooled_ref, other_ref, shard_ref, text_ref,
     fold, column, wbuf, bpart, tbuf, ibuf, pool2, grad2, qmat, pat, pbt,
-    gsend, gown, grecv, ysend, yown, yrecv, zsend, zrecv,
+    gsend, gterm, gown, grecv, ysend, yown, yrecv, zsend, zrecv,
     col_s, col_r, wy_s, wy_r, wx_s, wx_r, wsib_s, wsib_r,
     text_s, text_r, img_s, img_r, pair_s, pair_r,
-    gx_s, gx_r, gy_s, gy_r, gz_s, gz_r,
+    gx_s, gx_r, gy_s, gy_r, gz_s, gz_r, load_sem,
 ):
     nx, ny, nz = dims
     count = nx * ny * nz * 2
@@ -63,14 +69,23 @@
     def ring(step):
         return (me + step + count) % count
 
+    sent = []
+
     def send(src, dst, ssem, rsem, to):
         pltpu.make_async_remote_copy(
             src_ref=src, dst_ref=dst, send_sem=ssem, recv_sem=rsem, device_id=(to,), device_id_type=MESH
         ).start()
+        sent.append((src, ssem))
 
     def wait(ref, sem):
         pltpu.make_async_copy(ref, ref, sem).wait()
 
+    loads = [
+        pltpu.make_async_copy(src, dst, load_sem.at[k])
+        for k, (src, dst) in enumerate(
+            [(shard_hbm, shard_ref), (text_hbm, text_ref), (pooled_hbm, pooled_ref), (other_hbm, other_ref)]
+        )
+    ]
     ydist = ring_order(ny)
     xdist = ring_order(nx)
 
@@ -91,6 +106,10 @@
     for d in (-3, -2, -1, 1, 2, 3):
         hello(ring(d))
 
+    for load in loads:
+        load.start()
+
+    loads[0].wait()
     piece = shard_ref[...].astype(F32)
     fold[...] = jnp.zeros_like(fold)
     for r in range(TILES - 1):
@@ -99,26 +118,19 @@
     slot = c * nz + z
     column[slot] = fold[...].astype(BF16)
 
+    loads[1].wait()
     text = text_ref[...].astype(F32)
     text_inv = 1.0 / jnp.sqrt(jnp.sum(text * text, axis=1, keepdims=True) + EPS)
     tbuf[2] = (text * text_inv).astype(BF16)
+    loads[2].wait()
     pool2[c] = pooled_ref[...]
 
     pl.semaphore_wait(barrier, 2 * nz - 1 + len(ydist) + len(xdist) + 6)
 
-    def send_column(i, carry):
+    for i in range(1, 2 * nz):
         to = device(x, y, (z + i // 2) % nz, (c + i) % 2)
         send(column.at[slot], column.at[slot], col_s.at[i], col_r.at[slot], to)
-        return carry
-
-    lax.fori_loop(1, 2 * nz, send_column, 0)
-
-    send(tbuf.at[2], tbuf.at[4], text_s.at[0], text_r.at[4], ring(-2))
-    far = jnp.where(c == 0, -3, 1)
-    send(tbuf.at[2], tbuf.at[2 - far], text_s.at[1], text_r.at[2 - far], ring(far))
-    send(tbuf.at[2], tbuf.at[0], text_s.at[2], text_r.at[0], ring(2))
-    to_sib = 1 + 2 * c
-    send(tbuf.at[2], tbuf.at[to_sib], text_s.at[3], text_r.at[to_sib], sib)
+
     send(pool2.at[c], pool2.at[c], pair_s.at[0], pair_r.at[0], sib)
 
     j = lax.broadcasted_iota(jnp.int32, (kw, count), 0)
@@ -158,17 +170,39 @@
     def block(xx, yy):
         return wbuf.at[c, pl.ds(pl.multiple_of((xx * ny + yy) * rows, rows), rows), :]
 
+    right, left = (x + 1) % nx, (x + nx - 1) % nx
+    far = (x + 2) % nx
+    to_right, to_left, to_far = device(right, y, z, c), device(left, y, z, c), device(far, y, z, c)
+
     def share_x(yy, k):
-        for d in xdist:
-            send(block(x, yy), block(x, yy), wx_s.at[k, d], wx_r.at[x, yy], device((x + d) % nx, y, z, c))
-
+        send(block(x, yy), block(x, yy), wx_s.at[k, 0], wx_r.at[x, yy], to_right)
+        send(block(x, yy), block(x, yy), wx_s.at[k, 1], wx_r.at[x, yy], to_left)
+        if k in DIRECT:
+            send(block(x, yy), block(x, yy), wx_s.at[k, 2], wx_r.at[x, yy], to_far)
+
+    def pass_x(k):
+        yy = (y + yorder[k]) % ny
+        wait(block(left, yy), wx_r.at[left, yy])
+        wait(block(right, yy), wx_r.at[right, yy])
+        if k in BY_RIGHT:
+            send(block(left, yy), block(left, yy), wx_s.at[k, 2], wx_r.at[left, yy], to_right)
+        elif k not in DIRECT:
+            send(block(right, yy), block(right, yy), wx_s.at[k, 2], wx_r.at[right, yy], to_left)
+
+    yorder = [0] + ydist
     for d in ydist:
         send(block(x, y), block(x, y), wy_s.at[d], wy_r.at[y], device(x, (y + d) % ny, z, c))
     share_x(y, 0)
-    for d in ydist:
-        yy = (y + d) % ny
+    send(tbuf.at[2], tbuf.at[4], text_s.at[0], text_r.at[4], ring(-2))
+    send(tbuf.at[2], tbuf.at[0], text_s.at[1], text_r.at[0], ring(2))
+    to_sib = 1 + 2 * c
+    send(tbuf.at[2], tbuf.at[to_sib], text_s.at[2], text_r.at[to_sib], sib)
+    for k in range(1, ny):
+        yy = (y + yorder[k]) % ny
         wait(block(x, yy), wy_r.at[yy])
-        share_x(yy, d)
+        share_x(yy, k)
+        if k >= LAG:
+            pass_x(k - LAG)
 
     def whole(core, xx):
         return wbuf.at[core, pl.ds(pl.multiple_of(xx * span, span), span), :]
@@ -183,22 +217,28 @@
     pbt[...] = dot_t((jt == 3 * kt + 1).astype(F32).astype(BF16), both).astype(BF16)
 
     wait(tbuf.at[4], text_r.at[4])
+    wait(tbuf.at[0], text_r.at[0])
     pass_to = 3 + 2 * c
-    send(tbuf.at[4], tbuf.at[pass_to], text_s.at[4], text_r.at[pass_to], sib)
-
-    for d in xdist:
-        xx = (x + d) % nx
-        for yy in range(ny):
-            wait(block(xx, yy), wx_r.at[xx, yy])
-        send(whole(c, xx), whole(c, xx), wsib_s.at[d], wsib_r.at[xx], sib)
-    for d in [0] + xdist:
-        xx = (x + d) % nx
+    send(tbuf.at[4], tbuf.at[pass_to], text_s.at[3], text_r.at[pass_to], sib)
+    pass_from, pass_back = 4 - 4 * c, 5 - 4 * c
+    send(tbuf.at[pass_from], tbuf.at[pass_back], text_s.at[4], text_r.at[pass_back], ring(-1))
+
+    for k in range(ny - LAG, ny):
+        pass_x(k)
+    send(whole(c, left), whole(c, left), wsib_s.at[1], wsib_r.at[left], sib)
+    send(whole(c, right), whole(c, right), wsib_s.at[2], wsib_r.at[right], sib)
+    for k in range(ny):
+        yy = (y + yorder[k]) % ny
+        wait(block(far, yy), wx_r.at[far, yy])
+        send(block(far, yy), block(far, yy), wsib_s.at[3 + k], wsib_r.at[far], sib)
+    for xx in (x, left, right, far):
         wait(whole(1 - c, xx), wsib_r.at[xx])
 
     packed = wbuf[1, :, 2 * LANES :].astype(F32).reshape(nx * ny, rows, 5 * LANES)
     bpart[:, : 5 * LANES] = packed[:, :nz].reshape(chips, 5 * LANES).astype(BF16)
     bpart[:, 5 * LANES :] = packed[:, nz:, : 4 * LANES].reshape(chips, 4 * LANES).astype(BF16)
 
+    loads[3].wait()
     qa, qb = qmat[:, :count], qmat[:, count:]
     image = jnp.concatenate(
         [
@@ -212,11 +252,9 @@
     ibuf[3] = image_unit.astype(BF16)
 
     send(ibuf.at[3], ibuf.at[1], img_s.at[0], img_r.at[1], ring(2))
-    afar = jnp.where(c == 1, 3, -1)
-    send(ibuf.at[3], ibuf.at[3 - afar], img_s.at[1], img_r.at[3 - afar], ring(afar))
-    send(ibuf.at[3], ibuf.at[5], img_s.at[2], img_r.at[5], ring(-2))
+    send(ibuf.at[3], ibuf.at[5], img_s.at[1], img_r.at[5], ring(-2))
     img_sib = 2 + 2 * c
-    send(ibuf.at[3], ibuf.at[img_sib], img_s.at[3], img_r.at[img_sib], sib)
+    send(ibuf.at[3], ibuf.at[img_sib], img_s.at[2], img_r.at[img_sib], sib)
 
     temper = jnp.exp(jnp.full((1, 1), scale_ref[0], F32))
     bias = bias_ref[0]
@@ -229,7 +267,7 @@
         coef = (temper * sign / (1.0 + jnp.exp(-sign * logits))).astype(BF16)
         return dot(coef, blocks)
 
-    for k in (0, 1, 3, 5):
+    for k in (1, 3, 5):
         wait(tbuf.at[k], text_r.at[k])
     emb_grad = pairs(ibuf[3], tbuf[...].reshape(WINDOW * tok, D), 2)
     image_grad = (
@@ -250,31 +288,49 @@
         end = jnp.concatenate([full[:, HALF:], tail], axis=1).reshape(ny, nz, HALF)
         return jnp.concatenate([top, end], axis=1)
 
-    for d in xdist[::-1]:
-        xx = (x + d) % nx
-        gsend[d] = term(xx).astype(BF16)
-        for e in ydist + [0]:
-            yy = (y + e) % ny
-            send(gsend.at[d, yy], grecv.at[x, yy], gx_s.at[d, yy], gx_r.at[x, yy], device(xx, y, z, c))
+    gsend[0] = term(far).astype(BF16)
+    eorder = ydist[::-1] + [0]
+    for k, e in enumerate(eorder):
+        yy = (y + e) % ny
+        to = to_far if k in SUM_NONE else to_right if k in SUM_RIGHT else to_left
+        send(gsend.at[0, yy], grecv.at[2, yy], gx_s.at[0, yy], gx_r.at[2, yy], to)
+    gterm[0] = term(right)
+    gterm[1] = term(left)
+    for k, e in enumerate(eorder):
+        yy = (y + e) % ny
+        to_r, to_l = gterm[0, yy], gterm[1, yy]
+        if k not in SUM_NONE:
+            wait(grecv.at[2, yy], gx_r.at[2, yy])
+            passed = grecv[2, yy].astype(F32)
+            if k in SUM_RIGHT:
+                to_r += passed
+            else:
+                to_l += passed
+        gsend[1, yy] = to_r.astype(BF16)
+        gsend[2, yy] = to_l.astype(BF16)
+        send(gsend.at[1, yy], grecv.at[0, yy], gx_s.at[1, yy], gx_r.at[0, yy], to_right)
+        send(gsend.at[2, yy], grecv.at[1, yy], gx_s.at[2, yy], gx_r.at[1, yy], to_left)
     gown[...] = term(x)
 
     wait(ibuf.at[1], img_r.at[1])
+    wait(ibuf.at[5], img_r.at[5])
     img_pass = 2 * c
-    send(ibuf.at[1], ibuf.at[img_pass], img_s.at[4], img_r.at[img_pass], sib)
-
-    def sum_x(yy):
+    send(ibuf.at[1], ibuf.at[img_pass], img_s.at[3], img_r.at[img_pass], sib)
+    img_from, img_on = 5 - 4 * c, 4 - 4 * c
+    send(ibuf.at[img_from], ibuf.at[img_on], img_s.at[4], img_r.at[img_on], ring(1))
+
+    def sum_x(k, yy):
         total = gown[yy]
-        for d in xdist:
-            xx = (x + d) % nx
-            wait(grecv.at[xx, yy], gx_r.at[xx, yy])
-            total += grecv[xx, yy].astype(F32)
+        for n in (0, 1, 2) if k in SUM_NONE else (0, 1):
+            wait(grecv.at[n, yy], gx_r.at[n, yy])
+            total += grecv[n, yy].astype(F32)
         return total
 
-    for e in ydist:
+    for k, e in enumerate(eorder[:-1]):
         yy = (y + e) % ny
-        ysend[yy] = sum_x(yy).astype(BF16)
+        ysend[yy] = sum_x(k, yy).astype(BF16)
         send(ysend.at[yy], yrecv.at[y], gy_s.at[yy], gy_r.at[y], device(x, yy, z, c))
-    yown[...] = sum_x(y)
+    yown[...] = sum_x(ny - 1, y)
 
     own_grad = grad2[c]
     to_a = dot_t(own_grad[:, :HALF], wbuf[0]) + dot_t(own_grad[:, HALF:], wbuf[1, :, : 2 * LANES])
@@ -298,7 +354,7 @@
         zz = (z + e) % nz
         send(zrow(zz), zrecv.at[z], gz_s.at[zz], gz_r.at[z], device(x, y, zz, c))
 
-    for k in (0, 2, 4, 5):
+    for k in (0, 2, 4):
         wait(ibuf.at[k], img_r.at[k])
     text_emb_grad = pairs(tbuf[2], ibuf[...].reshape(WINDOW * tok, D), 3)
     text_again = text_ref[...].astype(F32)
@@ -315,30 +371,8 @@
         summed += zrecv[zz]
     weight_grad_ref[...] = summed
 
-    def sent_column(i, carry):
-        wait(column.at[slot], col_s.at[i])
-        return carry
-
-    lax.fori_loop(1, 2 * nz, sent_column, 0)
-    for k in range(5):
-        wait(tbuf.at[2], text_s.at[k])
-        wait(ibuf.at[3], img_s.at[k])
-    wait(pool2.at[c], pair_s.at[0])
-    wait(grad2.at[c], pair_s.at[1])
-    for d in ydist:
-        wait(block(x, y), wy_s.at[d])
-    for d in xdist:
-        for k in range(ny):
-            wait(block(x, y), wx_s.at[k, d])
-            wait(gsend.at[d, k], gx_s.at[d, k])
-    for d in [0] + xdist:
-        wait(whole(c, x), wsib_s.at[d])
-    for e in ydist:
-        yy = (y + e) % ny
-        wait(ysend.at[yy], gy_s.at[yy])
-    for e in ring_order(nz):
-        zz = (z + e) % nz
-        wait(zrow(zz), gz_s.at[zz])
+    for ref, sem in sent:
+        wait(ref, sem)
 
 
 def body(dims, pooled, other_part, head_weight, text, logit_scale, logit_bias):
@@ -348,6 +382,7 @@
     rows = 2 * nz
     dma = lambda *shape: pltpu.SemaphoreType.DMA(shape)
     vmem = pl.BlockSpec(memory_space=pltpu.VMEM)
+    hbm = pl.BlockSpec(memory_space=pltpu.HBM)
     smem = pl.BlockSpec(memory_space=pltpu.SMEM)
     pooled_grad, text_grad, total = pl.pallas_call(
         functools.partial(kernel, dims),
@@ -356,9 +391,13 @@
             jax.ShapeDtypeStruct((tok, D), F32),
             jax.ShapeDtypeStruct((16, LANES), F32),
         ),
-        in_specs=[vmem, vmem, vmem, vmem, smem, smem],
+        in_specs=[hbm, hbm, hbm, hbm, smem, smem],
         out_specs=(vmem, vmem, vmem),
         scratch_shapes=[
+            pltpu.VMEM((tok, kw), BF16),
+            pltpu.VMEM((tok, D), BF16),
+            pltpu.VMEM((1, GROUP), BF16),
+            pltpu.VMEM((tok, D), BF16),
             pltpu.VMEM((16, LANES), F32),
             pltpu.VMEM((rows, 16, LANES), BF16),
             pltpu.VMEM((2, count, HALF), BF16),
@@ -370,9 +409,10 @@
             pltpu.VMEM((tok, kw), BF16),
             pltpu.VMEM((count // 2, 2 * tok), BF16),
             pltpu.VMEM((count // 2, 2 * tok), BF16),
-            pltpu.VMEM((nx, ny, rows, HALF), BF16),
+            pltpu.VMEM((3, ny, rows, HALF), BF16),
+            pltpu.VMEM((2, ny, rows, HALF), F32),
             pltpu.VMEM((ny, rows, HALF), F32),
-            pltpu.VMEM((nx, ny, rows, HALF), BF16),
+            pltpu.VMEM((3, ny, rows, HALF), BF16),
             pltpu.VMEM((ny, rows, HALF), BF16),
             pltpu.VMEM((rows, HALF), F32),
             pltpu.VMEM((ny, rows, HALF), BF16),
@@ -380,17 +420,18 @@
             pltpu.VMEM((nz, 16, LANES), F32),
             dma(rows), dma(rows),
             dma(ny), dma(ny),
-            dma(ny, nx), dma(nx, ny),
-            dma(nx), dma(nx),
+            dma(ny, 3), dma(nx, ny),
+            dma(3 + ny), dma(nx),
             dma(5), dma(WINDOW),
             dma(5), dma(WINDOW),
             dma(2), dma(2),
-            dma(nx, ny), dma(nx, ny),
+            dma(3, ny), dma(3, ny),
             dma(ny), dma(ny),
             dma(nz), dma(nz),
+            dma(4),
         ],
         compiler_params=pltpu.CompilerParams(
-            collective_id=0, has_side_effects=True, vmem_limit_bytes=48 * 1024 * 1024
+            collective_id=0, has_side_effects=True, vmem_limit_bytes=60 * 1024 * 1024
         ),
     )(pooled, other_part, head_weight, text, logit_scale, logit_bias)
     flat = total[:TILES].reshape(1, TILES * LANES)

time: 81.6 us -> 76.6 us (0.939); the launches traced: 80.3 us -> 76.3 us
  Pallas kernels: 73.2 us -> 69.4 us
    pallas_call x1, Pallas kernels: 73.2 us -> 69.4 us  [body(): pl.pallas_call(functools.partial(kernel, dims), out_shape=(jax.ShapeDtype...]
    unnamed x12 -> x4, local copies, waits for them, and re-layouts: 4.35 us -> 4.24 us
where the time goes in v2:
time: 76.6 us; the launch traced here: 76.3 us
  Pallas kernels  69.4 us (91%)
  local copies, waits for them, and re-layouts  4.32 us (6%)
  between operations  1.95 us (3%)
    pallas_call x1, Pallas kernels, body(): pl.pallas_call(functools.partial(kernel, dims), out_shape=(jax.ShapeDtype...  69.4 us
    unnamed x4, local copies, waits for them, and re-layouts  4.24 us

profile of v2, /device:TPU:6, one launch (start us, length us, event | category | flops | bytes accessed | tf_op | source)
XLA Modules:
  0.0 76.3 jit_solution(16496160271908848914)
XLA Ops:
  1.9 69.4 %shard_map.85 = (bf16[128,768]{1,0:T(8,128)(2,1)}, f32[128,1152]{1,0:T(8,128)}, f32[16,128]{1,0:T(8,128)}) custom-call(bf16[128,768]{1,0:T(8,128)(2,1)} %pooled_hbm.1, bf16[128,1152]{1,0:T(8,128)(2,1)} %other_hbm.1, bf16[1,1728]{1,0:T(2,128)(2,1)} %shard_hbm.1, bf16[128,1152]{1,0:T(8,128)(2,1)} %text_hbm.1, f32[1]{0:T(128)S(6)} %copy.14.scale_ref, ...), custom_call_target="tpu_custom_call" | custom-call | tf_op jit(solution)/shard_map/pallas_call | solution.py:387
  71.3 0.7 slice_bitcast_fusion
  72.1 0.1 slice.17
  72.1 0.7 broadcast_select_fusion
  72.8 1.6 %copy.16 = bf16[128,768]{1,0:T(8,128)(2,1)} copy(bf16[128,768]{1,0:T(8,128)(2,1)} %get-tuple-element.12) | data formatting | bytes 393216
  74.4 1.9 %copy.17 = f32[128,1152]{1,0:T(8,128)} copy(f32[128,1152]{1,0:T(8,128)} %get-tuple-element.13) | data formatting | bytes 1179648
  (2 shorter events, 0.0 us)

commit v3 on v2

--- a/solution.py
+++ b/solution.py
@@ -40,13 +40,13 @@
 def kernel(
     dims,
     pooled_hbm, other_hbm, shard_hbm, text_hbm, scale_ref, bias_ref,
-    pooled_grad_ref, text_grad_ref, weight_grad_ref,
-    pooled_ref, other_ref, shard_ref, text_ref,
+    pooled_grad_hbm, text_grad_hbm, weight_grad_hbm,
+    pooled_ref, other_ref, shard_ref, text_ref, pooled_grad_ref, text_grad_ref, weight_grad_ref,
     fold, column, wbuf, bpart, tbuf, ibuf, pool2, grad2, qmat, pat, pbt,
     gsend, gterm, gown, grecv, ysend, yown, yrecv, zsend, zrecv,
     col_s, col_r, wy_s, wy_r, wx_s, wx_r, wsib_s, wsib_r,
     text_s, text_r, img_s, img_r, pair_s, pair_r,
-    gx_s, gx_r, gy_s, gy_r, gz_s, gz_r, load_sem,
+    gx_s, gx_r, gy_s, gy_r, gz_s, gz_r, load_sem, store_sem, ends_s, ends_r,
 ):
     nx, ny, nz = dims
     count = nx * ny * nz * 2
@@ -84,6 +84,12 @@
         pltpu.make_async_copy(src, dst, load_sem.at[k])
         for k, (src, dst) in enumerate(
             [(shard_hbm, shard_ref), (text_hbm, text_ref), (pooled_hbm, pooled_ref), (other_hbm, other_ref)]
+        )
+    ]
+    stores = [
+        pltpu.make_async_copy(src, dst, store_sem.at[k])
+        for k, (src, dst) in enumerate(
+            [(pooled_grad_ref, pooled_grad_hbm), (text_grad_ref, text_grad_hbm), (weight_grad_ref, weight_grad_hbm)]
         )
     ]
     ydist = ring_order(ny)
@@ -184,9 +190,11 @@
         yy = (y + yorder[k]) % ny
         wait(block(left, yy), wx_r.at[left, yy])
         wait(block(right, yy), wx_r.at[right, yy])
-        if k in BY_RIGHT:
+        if k in DIRECT:
+            pass
+        elif k in BY_RIGHT:
             send(block(left, yy), block(left, yy), wx_s.at[k, 2], wx_r.at[left, yy], to_right)
-        elif k not in DIRECT:
+        else:
             send(block(right, yy), block(right, yy), wx_s.at[k, 2], wx_r.at[right, yy], to_left)
 
     yorder = [0] + ydist
@@ -337,6 +345,8 @@
     to_b = dot_t(own_grad, bpart[...])
     pooled_grad_ref[...] = (dot_t(to_a.astype(BF16), pick_a) + dot_t(to_b.astype(BF16), pick_b)).astype(BF16)
 
+    stores[0].start()
+
     total = yown[...]
     for e in ydist:
         yy = (y + e) % ny
@@ -363,16 +373,40 @@
     text_grad_ref[...] = (
         text_emb_grad - text_unit * jnp.sum(text_unit * text_emb_grad, axis=1, keepdims=True)
     ) * again_inv
+    stores[1].start()
 
     summed = zsend[pl.ds(pl.multiple_of(z * 16, 16), 16), :]
     for e in ring_order(nz):
         zz = (z + e) % nz
         wait(zrecv.at[zz], gz_r.at[zz])
         summed += zrecv[zz]
-    weight_grad_ref[...] = summed
+    turned = pltpu.roll(summed, LANES // 2, 1)
+    low = lax.broadcasted_iota(jnp.int32, (1, LANES), 1) < LANES // 2
+    for b in range(TILES):
+        first, second = (9 + b) % TILES, (10 + b) % TILES
+        odd_row = jnp.where(low, turned[first : first + 1], turned[second : second + 1])
+        row_b = jnp.where(c == 0, summed[b : b + 1], odd_row)
+        width = min(LANES, GROUP - b * LANES)
+        weight_grad_ref[:, b * LANES : b * LANES + width] = row_b[:, :width]
+    stores[2].start()
 
     for ref, sem in sent:
         wait(ref, sem)
+    for store in stores:
+        store.wait()
+
+
+def finish_kernel(a, b, c, a_out, b_out, c_out, a_held, b_held, c_held, in_sem, out_sem):
+    parts = [(a, a_held, a_out), (b, b_held, b_out), (c, c_held, c_out)]
+    loads = [pltpu.make_async_copy(src, held, in_sem.at[k]) for k, (src, held, _) in enumerate(parts)]
+    stores = [pltpu.make_async_copy(held, dst, out_sem.at[k]) for k, (_, held, dst) in enumerate(parts)]
+    for load in loads:
+        load.start()
+    for load, store in zip(loads, stores):
+        load.wait()
+        store.start()
+    for store in stores:
+        store.wait()
 
 
 def body(dims, pooled, other_part, head_weight, text, logit_scale, logit_bias):
@@ -381,23 +415,25 @@
     tok, kw = pooled.shape
     rows = 2 * nz
     dma = lambda *shape: pltpu.SemaphoreType.DMA(shape)
-    vmem = pl.BlockSpec(memory_space=pltpu.VMEM)
     hbm = pl.BlockSpec(memory_space=pltpu.HBM)
     smem = pl.BlockSpec(memory_space=pltpu.SMEM)
-    pooled_grad, text_grad, total = pl.pallas_call(
+    made = pl.pallas_call(
         functools.partial(kernel, dims),
         out_shape=(
             jax.ShapeDtypeStruct((tok, kw), BF16),
             jax.ShapeDtypeStruct((tok, D), F32),
-            jax.ShapeDtypeStruct((16, LANES), F32),
+            jax.ShapeDtypeStruct((1, GROUP), F32),
         ),
         in_specs=[hbm, hbm, hbm, hbm, smem, smem],
-        out_specs=(vmem, vmem, vmem),
+        out_specs=(hbm, hbm, hbm),
         scratch_shapes=[
             pltpu.VMEM((tok, kw), BF16),
             pltpu.VMEM((tok, D), BF16),
             pltpu.VMEM((1, GROUP), BF16),
             pltpu.VMEM((tok, D), BF16),
+            pltpu.VMEM((tok, kw), BF16),
+            pltpu.VMEM((tok, D), F32),
+            pltpu.VMEM((1, GROUP), F32),
             pltpu.VMEM((16, LANES), F32),
             pltpu.VMEM((rows, 16, LANES), BF16),
             pltpu.VMEM((2, count, HALF), BF16),
@@ -429,16 +465,21 @@
             dma(ny), dma(ny),
             dma(nz), dma(nz),
             dma(4),
+            dma(3),
+            dma(4), dma(4),
         ],
         compiler_params=pltpu.CompilerParams(
             collective_id=0, has_side_effects=True, vmem_limit_bytes=60 * 1024 * 1024
         ),
     )(pooled, other_part, head_weight, text, logit_scale, logit_bias)
-    flat = total[:TILES].reshape(1, TILES * LANES)
-    first = flat[:, :GROUP]
-    second = jnp.concatenate([flat[:, D + 64 :], flat[:, :D]], axis=1)
-    weight_grad = jnp.where(lax.axis_index("dp") % 2 == 0, first, second)
-    return pooled_grad, text_grad, weight_grad
+    return pl.pallas_call(
+        finish_kernel,
+        out_shape=tuple(jax.ShapeDtypeStruct(m.shape, m.dtype) for m in made),
+        in_specs=[hbm, hbm, hbm],
+        out_specs=(hbm, hbm, hbm),
+        scratch_shapes=[pltpu.VMEM(m.shape, m.dtype) for m in made] + [dma(3), dma(3)],
+        compiler_params=pltpu.CompilerParams(vmem_limit_bytes=60 * 1024 * 1024),
+    )(*made)
 
 
 def solution(mesh, dims=(X, Y, Z)):

time: 76.6 us -> 73.3 us (0.957)
  local copies, waits for them, and re-layouts: 4.32 us -> 0 us
  Pallas kernels: 69.4 us -> 71.2 us
    unnamed x4 -> x0, local copies, waits for them, and re-layouts: 4.24 us -> none
    pallas_call x0 -> x1, Pallas kernels: none -> 2.04 us  [body(): pl.pallas_call(finish_kernel, out_shape=tuple((jax.ShapeDtypeStruct(m.sha...]
where the time goes in v3:
time: 73.3 us; the launch traced here: 73.1 us
  Pallas kernels  71.2 us (97%)
  between operations  1.93 us (3%)
    pallas_call x1, Pallas kernels, body(): pl.pallas_call(functools.partial(kernel, dims), out_shape=(jax.ShapeDtype...  69.1 us
    pallas_call x1, Pallas kernels, body(): pl.pallas_call(finish_kernel, out_shape=tuple((jax.ShapeDtypeStruct(m.sha...  2.04 us

profile of v3, /device:TPU:6, one launch (start us, length us, event | category | flops | bytes accessed | tf_op | source)
XLA Modules:
  0.0 73.1 jit_solution(2807260753536099070)
XLA Ops:
  1.9 69.1 %shard_map.85 = (bf16[128,768]{1,0:T(8,128)(2,1)}, f32[128,1152]{1,0:T(8,128)}, f32[1,1728]{1,0:T(1,128)}) custom-call(bf16[128,768]{1,0:T(8,128)(2,1)} %pooled_hbm.1, bf16[128,1152]{1,0:T(8,128)(2,1)} %other_hbm.1, bf16[1,1728]{1,0:T(2,128)(2,1)} %shard_hbm.1, bf16[128,1152]{1,0:T(8,128)(2,1)} %text_hbm.1, f32[1]{0:T(128)S(6)} %copy.9.scale_ref, ...), custom_call_target="tpu_custom_call" | custom-call | tf_op jit(solution)/shard_map/pallas_call | solution.py:420
  71.0 2.0 %shard_map.86 = (bf16[128,768]{1,0:T(8,128)(2,1)}, f32[128,1152]{1,0:T(8,128)}, f32[1,1728]{1,0:T(1,128)}) custom-call(bf16[128,768]{1,0:T(8,128)(2,1)} %get-tuple-element.6.a, f32[128,1152]{1,0:T(8,128)} %get-tuple-element.7.b, f32[1,1728]{1,0:T(1,128)} %get-tuple-element.8.c), custom_call_target="tpu_custom_call" | custom-call | tf_op jit(solution)/shard_map/pallas_call | solution.py:475

commit v4 on v3

--- a/solution.py
+++ b/solution.py
@@ -15,11 +15,11 @@
 WINDOW = 6
 X, Y, Z = 4, 8, 8
 EPS = 1e-06
-LAG = 2
+LAG = 3
 BY_RIGHT = (0, 2, 4)
-DIRECT = (5, 6, 7)
-SUM_RIGHT = (3, 5)
-SUM_NONE = (0, 1, 2)
+DIRECT = (6, 7)
+SUM_RIGHT = (3, 5, 7)
+SUM_NONE = (0, 1)
 F32 = jnp.float32
 BF16 = jnp.bfloat16
 MESH = pl.DeviceIdType.MESH

time: 73.3 us -> 72.2 us (0.985)
  Pallas kernels: 71.2 us -> 69.4 us
    pallas_call x1, Pallas kernels: 69.1 us -> 67.4 us  [body(): pl.pallas_call(functools.partial(kernel, dims), out_shape=(jax.ShapeDtype...]
where the time goes in v4:
time: 72.2 us; the launch traced here: 71.3 us
  Pallas kernels  69.4 us (96%)
  between operations  1.93 us (3%)
    pallas_call x1, Pallas kernels, body(): pl.pallas_call(functools.partial(kernel, dims), out_shape=(jax.ShapeDtype...  67.4 us
    pallas_call x1, Pallas kernels, body(): pl.pallas_call(finish_kernel, out_shape=tuple((jax.ShapeDtypeStruct(m.sha...  2.04 us

profile of v4, /device:TPU:6, one launch (start us, length us, event | category | flops | bytes accessed | tf_op | source)
XLA Modules:
  0.0 71.3 jit_solution(10909340805680065918)
XLA Ops:
  1.9 67.4 %shard_map.85 = (bf16[128,768]{1,0:T(8,128)(2,1)}, f32[128,1152]{1,0:T(8,128)}, f32[1,1728]{1,0:T(1,128)}) custom-call(bf16[128,768]{1,0:T(8,128)(2,1)} %pooled_hbm.1, bf16[128,1152]{1,0:T(8,128)(2,1)} %other_hbm.1, bf16[1,1728]{1,0:T(2,128)(2,1)} %shard_hbm.1, bf16[128,1152]{1,0:T(8,128)(2,1)} %text_hbm.1, f32[1]{0:T(128)S(6)} %copy.9.scale_ref, ...), custom_call_target="tpu_custom_call" | custom-call | tf_op jit(solution)/shard_map/pallas_call | solution.py:420
  69.3 2.0 %shard_map.86 = (bf16[128,768]{1,0:T(8,128)(2,1)}, f32[128,1152]{1,0:T(8,128)}, f32[1,1728]{1,0:T(1,128)}) custom-call(bf16[128,768]{1,0:T(8,128)(2,1)} %get-tuple-element.6.a, f32[128,1152]{1,0:T(8,128)} %get-tuple-element.7.b, f32[1,1728]{1,0:T(1,128)} %get-tuple-element.8.c), custom_call_target="tpu_custom_call" | custom-call | tf_op jit(solution)/shard_map/pallas_call | solution.py:475
